TPU v7x, 32 devices: a whole 2x2x4 slice. The times are simulated.
32 devices in a mesh: dp: 4 (over x, core), pts: 8 (over z, y).
Axes of the slice: x: 2, y: 2, z: 4, core: 2. Of those that a mesh axis runs over, the one named last changes fastest.
Arguments:
- samples_in: float32 [64, 2, 2048], P('dp', None, 'pts'), may hold values from -6 to 6, as said below
- target: float32 [64, 2048], P('dp', 'pts'), may hold values from -6 to 6
- mask: int32 [64, 2048], P('dp', 'pts'), may hold values from 0 to 1
- attn_w: float32 [2, 128, 512], replicated, may hold values from -0.5 to 0.5
- ffn_w: float32 [2, 2, 128, 256], replicated, may hold values from -0.5 to 0.5
- spec_w: float32 [2, 16, 2, 64, 64], replicated, may hold values from -0.5 to 0.5
- dense_w: float32 [320, 64], replicated, may hold values from -0.5 to 0.5
- vectors: float32 [1984], replicated, may hold values from -4 to 4, as said below
- attn_m: float32 [2, 128, 512], replicated
- ffn_m: float32 [2, 2, 128, 256], replicated
- spec_m: float32 [2, 16, 2, 64, 64], replicated
- dense_m: float32 [320, 64], replicated
- vector_m: float32 [1984], replicated
- attn_v: float32 [2, 128, 512], replicated, as said below
- ffn_v: float32 [2, 2, 128, 256], replicated, as said below
- spec_v: float32 [2, 16, 2, 64, 64], replicated, as said below
- dense_v: float32 [320, 64], replicated, as said below
- vector_v: float32 [1984], replicated, as said below
Outputs:
- loss_sum: float32 [], replicated
- valid_count: float32 [], replicated
- attn_m_new: float32 [2, 128, 512], replicated
- attn_v_new: float32 [2, 128, 512], replicated
- attn_w_new: float32 [2, 128, 512], replicated
- attn_w_low: bfloat16 [2, 128, 512], replicated
- ffn_m_new: float32 [2, 2, 128, 256], replicated
- ffn_v_new: float32 [2, 2, 128, 256], replicated
- ffn_w_new: float32 [2, 2, 128, 256], replicated
- ffn_w_low: bfloat16 [2, 2, 128, 256], replicated
- spec_m_new: float32 [2, 16, 2, 64, 64], replicated
- spec_v_new: float32 [2, 16, 2, 64, 64], replicated
- spec_w_new: float32 [2, 16, 2, 64, 64], replicated
- spec_w_low: bfloat16 [2, 16, 2, 64, 64], replicated
- dense_m_new: float32 [320, 64], replicated
- dense_v_new: float32 [320, 64], replicated
- dense_w_new: float32 [320, 64], replicated
- dense_w_low: bfloat16 [320, 64], replicated
- vector_m_new: float32 [1984], replicated
- vector_v_new: float32 [1984], replicated
- vector_w_new: float32 [1984], replicated
- vector_w_low: bfloat16 [1984], replicated
- weight_norms: float32 [8], replicated
- update_norms: float32 [8], replicated
- trust_ratios: float32 [8], replicated
Inputs may be any that keep to these rules, and one draw needn't show every extreme that they name: `samples_in`: row 1 holds the grid points' coordinates, rising by about 1 / 2048 from point to point. `vectors`: the norm gains are positive. `attn_v`: Positive. `ffn_v`: Positive. `spec_v`: Positive. `dense_v`: Positive. `vector_v`: Positive.
All inputs are finite; a program needn't handle non-finite values.
Results may differ from a plain program's by a relative error of at most 0.001.
Values sent between devices are 32-bit elements; how exact they have to be, the bound alone decides.
A program may use at most 192 MiB of HBM per device.

v0:
```python
import math

import jax
import jax.numpy as jnp
import ml_dtypes
import numpy as np
from jax import lax
from jax.experimental import pallas as pl
from jax.experimental.pallas import tpu as pltpu
from jax.sharding import PartitionSpec as P

D = 128
HEADS = 4
FF = 256
FREQ = 64
MODES = 16
LAYERS = 2
FLAYERS = 2
STEP = 5


HIGH = lax.Precision.HIGHEST
NORM_EPS = 1e-05
BETA_ONE = 0.5
BETA_TWO = 0.5
RATE = 0.2
DECAY = 0.01
ADAM_EPS = 1e-06


def vector_table():
    entries = [("lift_value", 0, D), ("lift_coord", 0, D), ("lift_bias", 0, D)]
    for layer in range(LAYERS):
        entries = entries + [
            ("key_gain", layer, D),
            ("value_gain", layer, D),
            ("inner_bias", layer, FF),
            ("outer_bias", layer, D),
        ]
    entries = entries + [("proj_bias", 0, FREQ)]
    for layer in range(FLAYERS):
        entries = entries + [("fourier_bias", layer, FREQ)]
    entries = entries + [("head_bias", 0, FREQ), ("head_out", 0, FREQ)]
    offsets = {}
    start = 0
    for label, layer, length in entries:
        offsets[label, layer] = (start, length)
        start = start + length
    return offsets


def pick(vectors, label, layer):
    start, length = vector_table()[label, layer]
    return vectors[start : start + length]


def head_norm(values, gain):
    centred = values - jnp.mean(values, -1, keepdims=True)
    scaled = centred * lax.rsqrt(jnp.mean(centred * centred, -1, keepdims=True) + NORM_EPS)
    return scaled * gain.reshape(HEADS, D // HEADS)


def lift(params, inputs):
    vectors = params[4]
    value = inputs[..., 0, :, None]
    coord = inputs[..., 1, :, None]
    return (
        value * pick(vectors, "lift_value", 0)
        + coord * pick(vectors, "lift_coord", 0)
        + pick(vectors, "lift_bias", 0)
    )


def attn_front(params, rows, layer, points):
    weight = params[0][layer]
    vectors = params[4]
    mixed = jnp.einsum("...d,de->...e", rows, weight[:, : 3 * D], precision=HIGH)
    shape = rows.shape[:-1] + (HEADS, D // HEADS)
    query = mixed[..., :D].reshape(shape)
    keys = head_norm(mixed[..., D : 2 * D].reshape(shape), pick(vectors, "key_gain", layer))
    values = head_norm(mixed[..., 2 * D :].reshape(shape), pick(vectors, "value_gain", layer))
    partial_sum = jnp.einsum("...phe,...phf->...hef", keys, values, precision=HIGH) / points
    return (query, partial_sum)


def attn_rear(params, rows, query, summary, layer):
    weight = params[0][layer]
    attended = jnp.einsum("...phe,...hef->...phf", query, summary, precision=HIGH).reshape(
        rows.shape
    )
    return rows + jnp.einsum("...d,de->...e", attended, weight[:, 3 * D :], precision=HIGH)


def ffn_block(params, rows, layer):
    weight = params[1][layer]
    vectors = params[4]
    inner = jnp.einsum("...d,df->...f", rows, weight[0], precision=HIGH) + pick(
        vectors, "inner_bias", layer
    )
    outer = jnp.einsum("...f,df->...d", jax.nn.gelu(inner), weight[1], precision=HIGH)
    return rows + outer + pick(vectors, "outer_bias", layer)


def project(params, rows):
    return jnp.einsum("...d,df->...f", rows, params[3][:D], precision=HIGH) + pick(
        params[4], "proj_bias", 0
    )


def mode_table(count, total):
    position = jnp.arange(count, dtype=jnp.int32)
    orders = jnp.arange(MODES, dtype=jnp.int32)
    phase = orders[:, None] * position[None, :] % total
    angle = phase.astype(jnp.float32) * (2.0 * math.pi / total)
    return jnp.concatenate([jnp.cos(angle), jnp.sin(angle)], 0)


def spectral_mix(coef, spec, first, width):
    columns = lax.dynamic_slice_in_dim(spec, first, width, 3)
    cosine = coef[..., :MODES, :]
    sine = coef[..., MODES:, :]
    real_part = columns[:, 0]
    imag_part = columns[:, 1]
    mixed_cos = jnp.einsum("...mf,mfg->...mg", cosine, real_part, precision=HIGH) + jnp.einsum(
        "...mf,mfg->...mg", sine, imag_part, precision=HIGH
    )
    mixed_sin = jnp.einsum("...mf,mfg->...mg", sine, real_part, precision=HIGH) - jnp.einsum(
        "...mf,mfg->...mg", cosine, imag_part, precision=HIGH
    )
    return jnp.concatenate([mixed_cos, mixed_sin], -2)


def fourier_end(params, back, rows, layer):
    local = params[3][D + layer * FREQ : D + (layer + 1) * FREQ]
    inner = back + jnp.einsum("...f,fg->...g", rows, local, precision=HIGH)
    return jax.nn.gelu(inner + pick(params[4], "fourier_bias", layer))


def head_loss(params, rows, target, mask_f):
    start = D + FLAYERS * FREQ
    hidden = jax.nn.gelu(
        jnp.einsum("...f,fg->...g", rows, params[3][start : start + FREQ], precision=HIGH)
        + pick(params[4], "head_bias", 0)
    )
    pred = jnp.einsum("...f,f->...", hidden, pick(params[4], "head_out", 0), precision=HIGH)
    diff = pred - target
    return jnp.sum(mask_f * diff * diff)


def add_all(first, second):
    return jax.tree.map(jnp.add, first, second)


def spectral_setup(points, parts):
    width = FREQ // parts
    return (mode_table(points, points), lax.axis_index("pts") * width, width, points)


def fourier_mix(spec, field, setup):
    grid, column, width, points = setup
    channel_rows = lax.all_to_all(field, "pts", split_axis=2, concat_axis=1, tiled=True)
    own_coef = jnp.einsum("kp,spc->skc", grid, channel_rows, precision=HIGH) / math.sqrt(points)
    full = lax.all_gather(own_coef, "pts", axis=2, tiled=True)
    mixed = spectral_mix(full, spec, column, width)
    spread = jnp.einsum("kp,skc->spc", grid, mixed, precision=HIGH) / math.sqrt(MODES)
    back = lax.all_to_all(spread, "pts", split_axis=1, concat_axis=2, tiled=True)
    return (back, full)


def fourier_back(params, grad_out, kept_item, layer, setup):
    field, full, back = kept_item
    grid, column, width, points = setup
    _, end_pull = jax.vjp(
        lambda weights, spread, inner: fourier_end(weights, spread, inner, layer),
        params,
        back,
        field,
    )
    grads, grad_back, grad_field = end_pull(grad_out)
    _, mix_pull = jax.vjp(
        lambda coef, weight: spectral_mix(coef, weight, column, width), full, params[2][layer]
    )
    grad_rows = lax.all_to_all(grad_back, "pts", split_axis=2, concat_axis=1, tiled=True)
    grad_mixed = jnp.einsum("kp,spc->skc", grid, grad_rows, precision=HIGH) / math.sqrt(MODES)
    grad_full, grad_spec = mix_pull(grad_mixed)
    grad_coef = lax.psum_scatter(grad_full, "pts", scatter_dimension=2, tiled=True)
    grad_chan = jnp.einsum("kp,skc->spc", grid, grad_coef, precision=HIGH) / math.sqrt(points)
    grad_field = grad_field + lax.all_to_all(
        grad_chan, "pts", split_axis=1, concat_axis=2, tiled=True
    )
    grads = (grads[0], grads[1], grads[2].at[layer].add(grad_spec), grads[3], grads[4])
    return (grads, grad_field)


def attention_back(params, grad_rows, kept_item, layer, points):
    rows, summary = kept_item
    (query, partial_sum), front_pull = jax.vjp(
        lambda weights, inner: attn_front(weights, inner, layer, points), params, rows
    )
    summary = lax.psum(partial_sum, "pts")
    middle, rear_pull = jax.vjp(
        lambda weights, inner, asked, summed: attn_rear(weights, inner, asked, summed, layer),
        params,
        rows,
        query,
        summary,
    )
    _, ffn_pull = jax.vjp(lambda weights, inner: ffn_block(weights, inner, layer), params, middle)
    ffn_grads, grad_middle = ffn_pull(grad_rows)
    rear_grads, grad_direct, grad_query, grad_summary = rear_pull(grad_middle)
    grad_summary = lax.psum(grad_summary, "pts")
    front_grads, grad_front = front_pull((grad_query, grad_summary))
    return (add_all(add_all(ffn_grads, rear_grads), front_grads), grad_direct + grad_front)


def lamb(weight, grad, first, second):
    first_new = BETA_ONE * first + (1.0 - BETA_ONE) * grad
    second_new = BETA_TWO * second + (1.0 - BETA_TWO) * grad * grad
    update = (
        first_new
        / (1.0 - BETA_ONE**STEP)
        / (jnp.sqrt(second_new / (1.0 - BETA_TWO**STEP)) + ADAM_EPS)
        + DECAY * weight
    )
    return (first_new, second_new, update)


def trust_step(weight, update, stacked):
    axes = tuple(range(1, weight.ndim)) if stacked else tuple(range(weight.ndim))
    weight_norm = jnp.sqrt(jnp.sum(weight * weight, axes))
    update_norm = jnp.sqrt(jnp.sum(update * update, axes))
    ratio = weight_norm / (update_norm + ADAM_EPS)
    scale = ratio.reshape(ratio.shape + (1,) * (weight.ndim - ratio.ndim))
    return (
        weight - RATE * scale * update,
        jnp.atleast_1d(weight_norm),
        jnp.atleast_1d(update_norm),
        jnp.atleast_1d(ratio),
    )


def finish(loss_sum, valid_count, params, grads, firsts, seconds):
    results = [loss_sum, valid_count]
    weight_norms, update_norms, ratios = ([], [], [])
    for weight, grad, first, second, stacked in zip(
        params, grads, firsts, seconds, (True, True, True, False, False)
    ):
        first_new, second_new, update = lamb(weight, grad, first, second)
        fresh, weight_norm, update_norm, ratio = trust_step(weight, update, stacked)
        results = results + [first_new, second_new, fresh, fresh.astype(jnp.bfloat16)]
        weight_norms.append(weight_norm)
        update_norms.append(update_norm)
        ratios.append(ratio)
    return results + [
        jnp.concatenate(weight_norms),
        jnp.concatenate(update_norms),
        jnp.concatenate(ratios),
    ]


def body(
    samples_in,
    target,
    mask,
    attn_w,
    ffn_w,
    spec_w,
    dense_w,
    vectors,
    attn_m,
    ffn_m,
    spec_m,
    dense_m,
    vector_m,
    attn_v,
    ffn_v,
    spec_v,
    dense_v,
    vector_v,
):
    params = (attn_w, ffn_w, spec_w, dense_w, vectors)
    parts = lax.axis_size("pts")
    local_pts = samples_in.shape[2]
    points = local_pts * parts
    mask_f = mask.astype(jnp.float32)
    valid_count = lax.psum(jnp.sum(mask_f), ("dp", "pts"))
    setup = spectral_setup(points, parts)
    rows, lift_pull = jax.vjp(lambda weights: lift(weights, samples_in), params)
    kept = []
    for layer in range(LAYERS):
        query, partial_sum = attn_front(params, rows, layer, points)
        summary = lax.psum(partial_sum, "pts")
        kept.append((rows, summary))
        rows = ffn_block(params, attn_rear(params, rows, query, summary, layer), layer)
    field, proj_pull = jax.vjp(project, params, rows)
    spectral_kept = []
    for layer in range(FLAYERS):
        back, full = fourier_mix(params[2][layer], field, setup)
        spectral_kept.append((field, full, back))
        field = fourier_end(params, back, field, layer)
    loss_part, head_pull = jax.vjp(
        lambda weights, inner: head_loss(weights, inner, target, mask_f), params, field
    )
    grads, grad_field = head_pull(1.0 / valid_count)
    for layer in reversed(range(FLAYERS)):
        layer_grads, grad_field = fourier_back(
            params, grad_field, spectral_kept[layer], layer, setup
        )
        grads = add_all(grads, layer_grads)
    proj_grads, grad_rows = proj_pull(grad_field)
    grads = add_all(grads, proj_grads)
    for layer in reversed(range(LAYERS)):
        layer_grads, grad_rows = attention_back(params, grad_rows, kept[layer], layer, points)
        grads = add_all(grads, layer_grads)
    grads = add_all(grads, lift_pull(grad_rows)[0])
    summed = lax.psum((grads[0], grads[1], grads[2], grads[3], grads[4], loss_part), ("dp", "pts"))
    out = finish(
        summed[5],
        valid_count,
        params,
        summed[:5],
        (attn_m, ffn_m, spec_m, dense_m, vector_m),
        (attn_v, ffn_v, spec_v, dense_v, vector_v),
    )
    return (
        out[0],
        out[1],
        out[2],
        out[3],
        out[4],
        out[5],
        out[6],
        out[7],
        out[8],
        out[9],
        out[10],
        out[11],
        out[12],
        out[13],
        out[14],
        out[15],
        out[16],
        out[17],
        out[18],
        out[19],
        out[20],
        out[21],
        out[22],
        out[23],
        out[24],
    )


F32 = jnp.float32
BF16 = jnp.bfloat16
ROWS = 1024
WIDE = 2048
NVEC_ROWS = 16


def dot(first, second, left=1, right=0, precision=None):
    return lax.dot_general(
        first,
        second,
        (((left,), (right,)), ((), ())),
        precision=precision,
        preferred_element_type=F32,
    )


def exact(first, second, left=1, right=0):
    return dot(first, second, left, right, HIGH)


def halves(value):
    high = value.astype(BF16)
    return high, (value - high.astype(F32)).astype(BF16)


def thirds(value):
    high = value.astype(BF16)
    rest = value - high.astype(F32)
    middle = rest.astype(BF16)
    return high, middle, (rest - middle.astype(F32)).astype(BF16)


def beside(*pieces):
    return jnp.concatenate(pieces, 1)


def above(*pieces):
    return jnp.concatenate(pieces, 0)


def fold(value):
    half = value.shape[1] // 2
    return value[:, :half] + value[:, half:]


def column_sum(value):
    rows, width = value.shape
    return jnp.sum(value.reshape(rows // 8, 8, width), 0)


def gelu_pair(inner):
    scale = math.sqrt(2.0 / math.pi)
    square = inner * inner
    bend = jnp.tanh(inner * (scale + (scale * 0.044715) * square))
    half = 0.5 + 0.5 * bend
    slope = half + (0.5 * inner) * (1.0 - bend * bend) * (scale + (3.0 * scale * 0.044715) * square)
    return inner * half, slope


def wide6_weight(weight):
    high, middle, low = thirds(weight)
    return above(high, high, middle, middle, low, high)


def wide6(pieces, weight):
    high, middle, low = pieces
    return dot(beside(high, middle, high, middle, high, low), weight)


def tall6_weight(weight):
    high, middle, low = thirds(weight)
    pair = beside(high, middle)
    return above(pair, pair), above(low, high)


def tall6(pieces, weights):
    high, middle, low = pieces
    return fold(dot(beside(high, middle), weights[0])) + dot(beside(high, low), weights[1])


def even4_weight(weight):
    high, low = halves(weight)
    pair = beside(high, low)
    return above(pair, pair)


def even4(pieces, weight):
    return fold(dot(beside(*pieces), weight))


def head_blocks(width):
    row = lax.broadcasted_iota(jnp.int32, (width, width), 0)
    column = lax.broadcasted_iota(jnp.int32, (width, width), 1)
    return row // (D // HEADS) == column // (D // HEADS)


def doubled(weight):
    zero = jnp.zeros_like(weight)
    return above(beside(weight, zero), beside(zero, weight))


MESH = pl.DeviceIdType.MESH


def position():
    dp, pts = lax.axis_index("dp"), lax.axis_index("pts")
    x, core, z, y = dp // 2, dp % 2, pts // 2, pts % 2
    return x, core, z, y


def device_of(x, core, z, y):
    return (2 * x + core, 2 * z + y)


def other(i):
    x, core, z, y = position()
    step = i + 1
    c = core + lax.div(step, 16) * (1 - 2 * core)
    x = x + lax.rem(lax.div(step, 8), 2) * (1 - 2 * x)
    y = y + lax.rem(lax.div(step, 4), 2) * (1 - 2 * y)
    z = lax.rem(z + lax.rem(step, 4), 4)
    return 16 * c + 8 * x + 4 * y + z, device_of(x, c, z, y)


def back_of(i):
    step = i + 1
    rest = lax.rem(step, 4)
    return step - rest + lax.rem(4 - rest, 4) - 1


def each_of(number, copy_of, start):
    def one(i, _):
        copy = copy_of(i)
        if start:
            copy.start()
        else:
            copy.wait()
        return 0

    lax.fori_loop(0, number, one, 0)


class Route:
    def __init__(self, rows, full, flat, landing, sends, receives, first):
        x, core, z, y = position()
        self.core, self.group = core, FLAYERS * MODES // 2
        self.rows, self.full, self.flat, self.landing = rows, full, flat, landing
        self.sends, self.receives, self.first = sends, receives, first
        self.peer = device_of(x, 1 - core, z, y)
        self.half, self.least = rows // 2, rows // (2 * self.group)
        self.own = (16 * core + 8 * x + 4 * y + z) * self.least

    def area(self, start, size):
        return pl.ds(pl.multiple_of(start, self.least), size)

    def link(self, source, target, slot, device):
        return pltpu.make_async_remote_copy(
            src_ref=source,
            dst_ref=target,
            send_sem=self.sends.at[self.first + slot],
            recv_sem=self.receives.at[self.first + slot],
            device_id=device,
            device_id_type=MESH,
        )

    def run(self, stage, start):
        half, least, core, group = self.half, self.least, self.core, self.group
        mine, yours = self.area(core * half, half), self.area((1 - core) * half, half)

        def copy_of(i):
            if stage == 0:
                return self.link(self.flat.at[yours], self.landing.at[pl.ds(0, half)], 2 * group - 1, self.peer)
            if stage == 3:
                return self.link(self.full.at[mine], self.full.at[mine if start else yours], 2 * group - 2, self.peer)
            number, device = other(i)
            if stage == 1:
                source = self.flat.at[self.area(number * least, least)]
                target = self.landing.at[self.area(half + i * least, least)]
            else:
                start_row = self.own if start else other(back_of(i))[0] * least
                source = self.full.at[self.area(self.own, least)]
                target = self.full.at[self.area(start_row, least)]
            return self.link(source, target, (stage - 1) * (group - 1) + i, device)

        if stage in (1, 2):
            each_of(group - 1, copy_of, start)
        elif start:
            copy_of(0).start()
        else:
            copy_of(0).wait()

    def start(self, stage):
        if stage == 2 and self.flat is not None:
            self.full[self.area(self.own, self.least), :] = self.flat[self.area(self.own, self.least), :]
        self.run(stage, True)

    def finish(self, stage):
        self.run(stage, False)
        if stage == 0:
            self.flat[self.area(self.core * self.half, self.half), :] += self.landing[: self.half, :]
        if stage == 1:
            mine = self.area(self.own, self.least)
            total = self.flat[mine, :]
            for i in range(self.group - 1):
                start = self.half + i * self.least
                total = total + self.landing[start : start + self.least, :]
            self.flat[mine, :] = total

    def step(self, stage):
        self.finish(stage)
        self.start(stage + 1)


def to_each(source_of, target, slot_of, mine, sends, receives, number, start):
    def copy_of(i):
        to, device = other(i)
        return pltpu.make_async_remote_copy(
            src_ref=source_of(to),
            dst_ref=target.at[slot_of(mine if start else other(back_of(i))[0])],
            send_sem=sends.at[i],
            recv_sem=receives.at[i],
            device_id=device,
            device_id_type=MESH,
        )

    each_of(number, copy_of, start)


def step_kernel(
    samples_ref,
    target_ref,
    mask_ref,
    attn_ref,
    ffn_ref,
    spec_any,
    turned_ref,
    vectors_ref,
    table_any,
    trow_any,
    early_any,
    late_out,
    mode_any,
    tail_out,
    spec_ref,
    table_ref,
    trow_ref,
    early_out,
    mode_out,
    local_sems,
    outgoing,
    incoming,
    vec_ref,
    early,
    early_land,
    late,
    late_land,
    mode_send,
    mode_land,
    tail_send,
    tail_swap,
    tail_pair,
    tail_land,
    route_send,
    route_recv,
    point_send,
    point_recv,
    mode_sends,
    mode_recvs,
    tail_sends,
    tail_recvs,
    lifted,
    lrows,
    w_kv,
    w_kvt,
    w_in,
    w_int,
    w0_u,
    mid_rows,
    w_out0,
    w_out1,
    w_outt,
    x_keep,
    r_keep,
    slope_keep,
    act_keep,
    mid_keep,
    h1_keep,
    h2_keep,
    z_keep,
    e_keep,
    s_acc,
    w0_kv,
    w0_g,
    n_keep,
    small_keep,
    nt_keep,
    cent_keep,
    coef_acc,
    coef_keep,
    stack_ref,
    sq_acc,
    p_acc,
    w2_acc,
    w1_acc,
    kv_acc,
    v_acc,
    u_acc,
    vt_acc,
    b_acc,
    d_keep,
    t_keep,
    wz,
):
    parts = samples_ref.shape[0] // 2
    count = 2
    points = samples_ref.shape[2] * parts
    devices = FLAYERS * MODES
    x, core, z, y = position()
    pts = 2 * z + y
    place = 8 * x + 4 * y + z
    mine = 16 * core + place
    early_route = Route(early.shape[0], early_out, early, early_land, route_send, route_recv, 0)
    late_route = Route(late.shape[0], late_out, late, late_land, route_send, route_recv, devices)
    mode_route = Route(mode_out.shape[0], mode_out, None, None, route_send, route_recv, 2 * devices)

    barrier = pltpu.get_barrier_semaphore()
    take = [
        pltpu.make_async_copy(source, target, local_sems.at[i])
        for i, (source, target) in enumerate(((trow_any, trow_ref), (spec_any, spec_ref), (table_any, table_ref)))
    ]
    put_mode = pltpu.make_async_copy(mode_out, mode_any, local_sems.at[3])
    put_early = pltpu.make_async_copy(early_out, early_any, local_sems.at[4])
    for copy in take:
        copy.start()

    def greet(i, _):
        pl.semaphore_signal(barrier, inc=1, device_id=other(i)[1], device_id_type=MESH)
        return 0

    lax.fori_loop(0, devices - 1, greet, 0)
    for p in range(parts):
        outgoing[p, 0:2, :] = samples_ref[2 * p]
        outgoing[p, 2:4, :] = samples_ref[2 * p + 1]
        outgoing[p, 4:6, :] = target_ref[2 * p : 2 * p + 2, :]
        outgoing[p, 6:8, :] = mask_ref[2 * p : 2 * p + 2, :].astype(F32)
    incoming[pts] = outgoing[pts]
    for i in range(NVEC_ROWS - 1):
        vec_ref[i : i + 1, :] = vectors_ref[i * D : (i + 1) * D].reshape(1, D)
    last = vectors_ref.shape[0] - (NVEC_ROWS - 1) * D
    vec_ref[NVEC_ROWS - 1 :, :last] = vectors_ref[(NVEC_ROWS - 1) * D :].reshape(1, last)
    total = count * points
    steps = points // ROWS
    rows_all = total // ROWS
    blocks = head_blocks(D)
    block_f = jnp.where(blocks, 1.0, 0.0).astype(F32)
    block_b = block_f.astype(BF16)
    mean_weight = above(block_b, block_b)
    centre = (
        jnp.where(
            lax.broadcasted_iota(jnp.int32, (D, D), 0) == lax.broadcasted_iota(jnp.int32, (D, D), 1),
            1.0,
            0.0,
        ).astype(F32)
        - block_f * (HEADS / D)
    )
    eye = jnp.where(
        lax.broadcasted_iota(jnp.int32, (D, D), 0) == lax.broadcasted_iota(jnp.int32, (D, D), 1), 1.0, 0.0
    ).astype(F32)

    def vector(label, layer):
        start, length = vector_table()[label, layer]
        if length == 2 * D:
            row = start // D
            return beside(vec_ref[row : row + 1, :], vec_ref[row + 1 : row + 2, :])
        row = start // D
        if length == D:
            return vec_ref[row : row + 1, :]
        offset = start - row * D
        piece = vec_ref[row : row + 1, offset : offset + FREQ]
        return beside(piece, piece)

    def block(index):
        return pl.ds(pl.multiple_of(index * ROWS, ROWS), ROWS)

    wide_steps = points // WIDE

    def wide_block(index):
        return pl.ds(pl.multiple_of(index * WIDE, WIDE), WIDE)

    lift_rows = above(
        vector("lift_value", 0), vector("lift_coord", 0), vector("lift_bias", 0), jnp.zeros((5, D), F32)
    )

    def lift_weight(mixed):
        high, middle, low = [item.astype(F32) for item in thirds(mixed)]
        parts = []
        for i in range(2):
            hi, mi, lo = high[i : i + 1], middle[i : i + 1], low[i : i + 1]
            parts += [hi, hi, mi, mi, lo, hi]
        parts += [high[2:3], middle[2:3], low[2:3]]
        parts.append(jnp.zeros((D - 15, mixed.shape[1]), F32))
        return above(*parts).astype(BF16)

    def point_copy(k, start):
        other = lax.rem(pts + k, parts)
        sender = lax.rem(pts + parts - k, parts)
        return pltpu.make_async_remote_copy(
            src_ref=outgoing.at[other],
            dst_ref=incoming.at[pts if start else sender],
            send_sem=point_send.at[k - 1],
            recv_sem=point_recv.at[k - 1],
            device_id=(2 * x + core, other),
            device_id_type=MESH,
        )

    for layer in range(LAYERS):
        if layer == 1:
            pl.semaphore_wait(barrier, devices - 1)
            for k in range(1, parts):
                point_copy(k, True).start()
        weight = attn_ref[layer]
        keyed = beside(exact(weight[:, D : 2 * D], centre), exact(weight[:, 2 * D : 3 * D], centre))
        cent_keep[layer] = keyed
        if layer == 0:
            w0_kv[...] = lift_weight(exact(lift_rows, keyed))
        else:
            w_kv[...] = wide6_weight(keyed)
            pair, rest = tall6_weight(keyed.T)
            w_kvt[:, : 2 * D] = pair
            w_kvt[:, 2 * D :] = rest
        first, second = ffn_ref[layer, 0], ffn_ref[layer, 1]
        if layer:
            w_in[...] = wide6_weight(first)
            pair, rest = tall6_weight(first.T)
            w_int[:, : 2 * D] = pair
            w_int[:, 2 * D :] = rest
        pair, rest = tall6_weight(second.T)
        w_out0[layer] = pair
        w_out1[layer] = rest
        w_outt[layer] = wide6_weight(second)

    s_acc[...] = jnp.zeros_like(s_acc)
    coef_acc[...] = jnp.zeros_like(coef_acc)
    sq_acc[...] = jnp.zeros_like(sq_acc)
    p_acc[...] = jnp.zeros_like(p_acc)
    w2_acc[...] = jnp.zeros_like(w2_acc)
    w1_acc[...] = jnp.zeros_like(w1_acc)
    kv_acc[...] = jnp.zeros_like(kv_acc)
    v_acc[...] = jnp.zeros_like(v_acc)
    u_acc[...] = jnp.zeros_like(u_acc)
    vt_acc[...] = jnp.zeros_like(vt_acc)
    b_acc[...] = jnp.zeros_like(b_acc)

    for k in range(1, parts):
        point_copy(k, False).wait()
    whole = beside(*[incoming[p] for p in range(parts)])
    for s in range(count):
        value, coord = whole[2 * s : 2 * s + 1], whole[2 * s + 1 : 2 * s + 2]
        target, valid = whole[4 + s : 5 + s], whole[6 + s : 7 + s]
        one = jnp.ones_like(value)
        vh, vm, vl = [item.astype(F32) for item in thirds(value)]
        ch, cm, cl = [item.astype(F32) for item in thirds(coord)]
        th, tm, tl = [item.astype(F32) for item in thirds(target)]
        zero = jnp.zeros((D - 19, points), F32)
        stack = above(vh, vm, vh, vm, vh, vl, ch, cm, ch, cm, ch, cl, one, one, one, th, tm, tl, valid, zero)
        lifted[s * points : (s + 1) * points, :] = stack.T.astype(BF16)
        short = above(vh, vm, vl, ch, cm, cl, one, jnp.zeros((9, points), F32)).astype(BF16)
        for i in range(steps):
            lrows[s * steps + i] = short[:, i * ROWS : (i + 1) * ROWS]

    def head_scale(centred):
        high, low = halves(centred * centred)
        var = beside(
            dot(beside(high[:, :D], low[:, :D]), mean_weight), dot(beside(high[:, D:], low[:, D:]), mean_weight)
        )
        return lax.rsqrt(var * (HEADS / D) + NORM_EPS)

    def normalise(layer, where, s, centred):
        scale = head_scale(centred)
        normal = centred * scale
        if layer:
            x_keep[where, :] = normal
            r_keep[where, :] = scale
        high, low = halves(normal)
        s_acc[s] += dot(
            beside(high[:, :D], low[:, :D]), beside(high[:, D:], low[:, D:]), 0, 0
        )

    def quarters(value):
        half_row, half_col = value.shape[0] // 2, value.shape[1] // 2
        return (
            value[:half_row, :half_col]
            + value[half_row:, :half_col]
            + (value[:half_row, half_col:] + value[half_row:, half_col:])
        )

    def summarise(layer):
        weight = attn_ref[layer]
        key_gain = vector("key_gain", layer).reshape(1, D)
        value_gain = vector("value_gain", layer).reshape(1, D)
        key_column = jnp.sum(eye * key_gain, 1, keepdims=True)
        for s in range(count):
            plain = jnp.where(blocks, quarters(s_acc[s]), 0.0) * (1.0 / points)
            summary = key_column * plain * value_gain
            mixed = exact(summary, weight[:, 3 * D :])
            both = exact(weight[:, :D], mixed)
            n_keep[layer, s] = both
            small_keep[layer, s, 0] = plain
            small_keep[layer, s, 1] = summary
            small_keep[layer, s, 2] = mixed
            if layer == 0:
                rows = exact(lift_rows, eye + both)
                mid_rows[s] = rows
                w0_g[s] = lift_weight(rows)
                w0_u[s] = lift_weight(exact(rows, ffn_ref[0, 0]))
            else:
                pair, rest = tall6_weight(both)
                wz[s, : 2 * D, :] = pair
                wz[s, 2 * D :, :D] = rest
                nt_keep[s] = even4_weight(both.T)

    def feed(layer, index, mid, inner):
        where = block(index)
        act, slope = gelu_pair(inner + vector("inner_bias", layer))
        slope_keep[layer, where, :] = slope
        pieces = thirds(act)
        act_keep[layer, where, :] = beside(pieces[0], pieces[1])
        return mid + tall6(pieces, (w_out0[layer], w_out1[layer])) + vector("outer_bias", layer)

    def front_zero(index, _):
        where = wide_block(index)
        normalise(0, where, index // wide_steps, dot(lifted[where, :], w0_kv[...]))
        return 0

    lax.fori_loop(0, count * wide_steps, front_zero, 0)
    summarise(0)
    s_acc[...] = jnp.zeros_like(s_acc)

    def layer_zero(index, _):
        where = block(index)
        s = index // steps
        data = lifted[where, :]
        out = feed(0, index, dot(data, w0_g[s]), dot(data, w0_u[s]))
        d_keep[where, :] = out
        pieces = thirds(out)
        h1_keep[where, :] = beside(pieces[0], pieces[1])
        h2_keep[where, 2 * D :] = pieces[2]
        normalise(1, where, s, wide6(pieces, w_kv[...]))
        return 0

    lax.fori_loop(0, rows_all, layer_zero, 0)
    summarise(1)
    s_acc[...] = jnp.zeros_like(s_acc)

    def pieces_of(ref, where, number=3):
        value = ref[where, : number * D]
        return [value[:, i * D : (i + 1) * D] for i in range(number)]

    def layer_one(index, _):
        where = block(index)
        s = index // steps
        pieces = pieces_of(h1_keep, where, 2) + [h2_keep[where, 2 * D :]]
        mid = d_keep[where, :] + tall6(pieces, (wz[s, : 2 * D, :], wz[s, 2 * D :, :D]))
        pieces = thirds(mid)
        mid_keep[where, :] = beside(pieces[0], pieces[1])
        out = feed(1, index, mid, wide6(pieces, w_in[...]))
        h2_keep[where, :] = beside(*thirds(out))
        return 0

    lax.fori_loop(0, rows_all, layer_one, 0)

    def dense_rows(part):
        start = D + (part - 1) * FREQ if part else 0
        return turned_ref[:, start : start + (FREQ if part else D)].T

    proj0, proj1 = tall6_weight(doubled(dense_rows(0)))
    locals6 = [tall6_weight(doubled(dense_rows(part))) for part in (1, 2, 3)]
    turned6 = [tall6_weight(doubled(dense_rows(part).T)) for part in (1, 2, 3)]
    own = lax.broadcasted_iota(jnp.int32, (2 * count * MODES, MODES * D), 1) // D == lax.rem(
        lax.broadcasted_iota(jnp.int32, (2 * count * MODES, MODES * D), 0), MODES
    )

    def mode_rows(coef):
        cosine, sine = coef[:MODES], coef[MODES:]
        c = [cosine[:, s * FREQ : (s + 1) * FREQ] for s in range(count)]
        d = [sine[:, s * FREQ : (s + 1) * FREQ] for s in range(count)]
        return above(
            *[beside(c[s], d[s]) for s in range(count)], *[beside(d[s], -c[s]) for s in range(count)]
        )

    def spread_rows(rows):
        return jnp.where(own, beside(*([rows] * MODES)), 0.0)

    def unpack(rows):
        lead = count * MODES
        return above(
            *[beside(*[rows[j * lead + s * MODES : j * lead + (s + 1) * MODES] for s in range(count)]) for j in (0, 1)]
        )

    def pack(value):
        return above(
            *[
                value[j * MODES : (j + 1) * MODES, s * FREQ : (s + 1) * FREQ]
                for j in (0, 1)
                for s in range(count)
            ]
        )

    def set_stack(value):
        high, middle, low = thirds(value)
        stack_ref[...] = above(
            high, high, middle, middle, low, high, jnp.zeros((4 * MODES, D), BF16)
        )

    def take_coef(index, high, low):
        both = beside(high, low)
        each = both.shape[0] // ROWS
        for i in range(each):
            coef_acc[...] += dot(trow_ref[index * each + i], both[i * ROWS : (i + 1) * ROWS])

    def mix_forward(layer):
        coef = quarters(coef_acc[...]) * (1.0 / math.sqrt(points))
        coef_acc[...] = jnp.zeros_like(coef_acc)
        rows = mode_rows(coef)
        coef_keep[layer] = rows
        set_stack(unpack(exact(spread_rows(rows), spec_ref[layer])) * (1.0 / math.sqrt(MODES)))

    def mix_back(layer):
        cot = pack(quarters(coef_acc[...])) * (1.0 / math.sqrt(MODES))
        coef_acc[...] = jnp.zeros_like(coef_acc)
        kept_rows = coef_keep[layer]
        padded = beside(cot, jnp.zeros_like(cot))
        for k in range(MODES):
            for r in range(2 * count):
                mode_send[layer * MODES + k, r : r + 1, :] = kept_rows[r * MODES + k : r * MODES + k + 1]
                mode_send[layer * MODES + k, 4 + r : 5 + r, :] = padded[r * MODES + k : r * MODES + k + 1]
        wide = jnp.where(own, exact(cot, spec_ref[layer], 1, 1), 0.0)
        kept = wide[:, :D]
        for k in range(1, MODES):
            kept = kept + wide[:, k * D : (k + 1) * D]
        lead = count * MODES
        first, second = kept[:lead], kept[lead:]
        rows = above(first[:, :FREQ] - second[:, FREQ:], first[:, FREQ:] + second[:, :FREQ])
        set_stack(unpack(rows) * (1.0 / math.sqrt(points)))

    def project_step(index, _):
        where = wide_block(index)
        first = h2_keep[wide_block(index), :]
        second = h2_keep[wide_block(index + wide_steps), :]
        pieces = [beside(first[:, i * D : (i + 1) * D], second[:, i * D : (i + 1) * D]) for i in range(3)]
        field = tall6(pieces, (proj0, proj1)) + vector("proj_bias", 0)
        pieces = thirds(field)
        z_keep[0, where, :] = beside(*pieces)
        take_coef(index, pieces[0], pieces[1])
        return 0

    for copy in take:
        copy.wait()
    lax.fori_loop(0, wide_steps, project_step, 0)
    mix_forward(0)

    def fourier_field(layer, where):
        pieces = pieces_of(z_keep.at[layer], where)
        inner = dot(table_ref[where, :], stack_ref[...]) + (
            tall6(pieces, locals6[layer]) + vector("fourier_bias", layer)
        )
        return gelu_pair(inner)

    def fourier_one(index, _):
        where = wide_block(index)
        field, slope = fourier_field(0, where)
        d_keep[where, :] = slope
        pieces = thirds(field)
        z_keep[1, where, :] = beside(*pieces)
        take_coef(index, pieces[0], pieces[1])
        return 0

    lax.fori_loop(0, wide_steps, fourier_one, 0)
    mix_forward(1)

    lane = lax.broadcasted_iota(jnp.int32, (2 * D, 2 * D), 1)
    row = lax.broadcasted_iota(jnp.int32, (2 * D, 2 * D), 0)
    inner_row = lax.rem(row, D)
    same = row // D == lax.rem(lane, D) // FREQ
    pick_target = (lane < D) & (inner_row >= 15) & (inner_row < 18)
    pick_mask = (lane >= D) & (inner_row == 18)
    spread = jnp.where(same & (pick_target | pick_mask), 1.0, 0.0).astype(BF16)
    out_row = vector("head_out", 0)
    out_column = jnp.sum(eye * out_row, 1, keepdims=True)
    half_blocks = (
        lax.broadcasted_iota(jnp.int32, (D, D), 0) // FREQ == lax.broadcasted_iota(jnp.int32, (D, D), 1) // FREQ
    )
    out_weight = tall6_weight(jnp.where(half_blocks, out_column, 0.0))

    def pair_product(first, second):
        return dot(beside(*first), beside(*second), 0, 0)

    def loss_step(index, _):
        where = block(index)
        field, slope = fourier_field(1, where)
        pieces = thirds(field)
        hidden, hidden_slope = gelu_pair(tall6(pieces, locals6[2]) + vector("head_bias", 0))
        pred = tall6(thirds(hidden), out_weight)
        known = dot(beside(lifted[where, :], lifted[block(index + steps), :]), spread)
        diff = pred - known[:, :D]
        valid = known[:, D:]
        cot = (2.0 * valid) * diff
        b_acc[0:8, :D] += column_sum(valid * diff * diff)
        b_acc[8:16, :D] += column_sum(valid)
        b_acc[16:24, :D] += column_sum(hidden * cot)
        cot = cot * out_row * hidden_slope
        b_acc[24:32, :D] += column_sum(cot)
        split = thirds(cot)
        sq_acc[2] += pair_product(pieces[:2], split[:2])
        cot = tall6(split, turned6[2]) * slope
        b_acc[32:40, :D] += column_sum(cot)
        split = thirds(cot)
        e_keep[where, :] = beside(*split)
        sq_acc[1] += pair_product(pieces_of(z_keep.at[1], where, 2), split[:2])
        take_coef(index, *split[:2])
        return 0

    lax.fori_loop(0, steps, loss_step, 0)
    mix_back(1)

    def fourier_cot(layer, where):
        return tall6(pieces_of(e_keep, where), turned6[layer]) + dot(table_ref[where, :], stack_ref[...])

    def fourier_back(index, _):
        where = wide_block(index)
        cot = fourier_cot(1, where) * d_keep[where, :]
        b_acc[40:48, :D] += column_sum(cot)
        split = thirds(cot)
        e_keep[where, :] = beside(*split)
        sq_acc[0] += pair_product(pieces_of(z_keep.at[0], where, 2), split[:2])
        take_coef(index, *split[:2])
        return 0

    lax.fori_loop(0, wide_steps, fourier_back, 0)
    mix_back(0)
    mode_land[mine] = mode_send[mine]
    to_each(lambda r: mode_send.at[r], mode_land, lambda r: r, mine, mode_sends, mode_recvs, devices - 1, True)
    proj_back = wide6_weight(doubled(turned_ref[:, :D]))

    def project_back(index, _):
        where = wide_block(index)
        later = wide_block(index + wide_steps)
        cot = fourier_cot(0, where)
        b_acc[48:56, :D] += column_sum(cot)
        split = thirds(cot)
        first = pieces_of(h2_keep, where, 2)
        second = pieces_of(h2_keep, later, 2)
        p_acc[...] += dot(beside(first[0], second[0], first[1], second[1]), beside(*split[:2]), 0, 0)
        rows = wide6(split, proj_back)
        d_keep[where, :] = rows[:, :D]
        d_keep[later, :] = rows[:, D:]
        return 0

    lax.fori_loop(0, wide_steps, project_back, 0)

    def feed_back(layer, index, cot):
        where = block(index)
        base = 56 + layer * 16
        b_acc[base : base + 8, :D] += column_sum(cot)
        split = thirds(cot)
        act = act_keep[layer, where, :]
        w2_acc[layer] += dot(beside(*split[:2]), act[:, :FF], 0, 0)
        w2_acc[layer, :D, :] += dot(split[0], act[:, FF:], 0, 0)
        inner = wide6(split, w_outt[layer]) * slope_keep[layer, where, :]
        b_acc[base + 8 : base + 16, :] += column_sum(inner)
        return split, thirds(inner)

    def layer_one_back(index, _):
        @pl.when(index == 1)
        def _():
            to_each(lambda r: mode_send.at[r], mode_land, lambda r: r, mine, mode_sends, mode_recvs, devices - 1, False)
            landed = mode_land[...].reshape(devices * 8, D)
            shifted = above(landed[4:], landed[:4])
            row = lax.broadcasted_iota(jnp.int32, landed.shape, 0)
            product = exact(jnp.where(lax.rem(row, 8) < 4, landed, 0.0), shifted[:, :FREQ], 0, 0)
            mode_out[mode_route.area(mode_route.own, FREQ), :] = beside(product[:FREQ], product[FREQ:])
            mode_route.start(2)

        where = block(index)
        cot = d_keep[where, :]
        _, pieces = feed_back(1, index, cot)
        high, low = pieces[:2]
        mid = mid_keep[where, :]
        w1_acc[...] += dot(mid, high, 0, 0)
        w1_acc[:D, :] += dot(mid[:, :D], low, 0, 0)
        cot = cot + tall6(pieces, (w_int[:, : 2 * D], w_int[:, 2 * D :]))
        d_keep[where, :] = cot
        s_acc[index // steps] += pair_product(pieces_of(h1_keep, where, 2), halves(cot))
        return 0

    lax.fori_loop(0, rows_all, layer_one_back, 0)

    def attend_back(layer, products):
        weight = attn_ref[layer]
        query, outer = weight[:, :D], weight[:, 3 * D :]
        key_gain, value_gain = vector("key_gain", layer), vector("value_gain", layer)
        key_column = jnp.sum(eye * key_gain, 1, keepdims=True)
        key_total = jnp.zeros((D, 1), F32)
        value_total = jnp.zeros((1, D), F32)
        query_grad = jnp.zeros((D, D), F32)
        outer_grad = jnp.zeros((D, D), F32)
        for s in range(count):
            plain, summary, mixed = small_keep[layer, s, 0], small_keep[layer, s, 1], small_keep[layer, s, 2]
            turned = exact(query, products[s], 0, 0)
            outer_grad += exact(summary, turned, 0, 0)
            if layer:
                query_grad += exact(products[s], mixed, 1, 1)
            cot = jnp.where(blocks, exact(turned, outer, 1, 1), 0.0)
            both = cot * plain
            key_total += jnp.sum(both * value_gain, 1, keepdims=True)
            value_total += jnp.sum(both * key_column, 0, keepdims=True)
            scaled = key_column * cot * value_gain * (1.0 / points)
            t_keep[s, 0] = even4_weight(scaled.T)
            t_keep[s, 1] = even4_weight(scaled)
        if layer:
            early[5 * D + FREQ : 6 * D + FREQ, :] = query_grad
            early[6 * D + FREQ : 7 * D + FREQ, :] = outer_grad
        else:
            late[6 * D : 7 * D, :] = outer_grad
        return jnp.sum(eye * key_total, 0, keepdims=True), value_total

    for i in range(2):
        half = slice(i * D, (i + 1) * D)
        early[i * D : (i + 1) * D, :] = w1_acc[:D, half] + w1_acc[D:, half]
        early[(2 + i) * D : (3 + i) * D, :] = w2_acc[1, :D, half] + w2_acc[1, D:, half]
    sums = p_acc[...]
    sums = fold(sums[: 2 * D] + sums[2 * D :])
    early[4 * D : 4 * D + FREQ, :] = (sums[:D, :FREQ] + sums[D:, FREQ:]).T
    squares = []
    for part in range(3):
        sums = quarters(sq_acc[part])
        squares.append((sums[:FREQ, :FREQ] + sums[FREQ:, FREQ:]).T)
    early[4 * D + FREQ : 5 * D, :] = beside(squares[0], squares[1])
    early[5 * D : 5 * D + FREQ, :] = beside(squares[2], jnp.zeros_like(squares[2]))
    early[7 * D + FREQ :, :] = jnp.zeros((D // 2, D), F32)
    gains = [None, None]
    gains[1] = attend_back(1, [quarters(s_acc[s]) for s in range(count)])

    def norm_back(s, normal, scale):
        key, value = normal[:, :D], normal[:, D:]
        key_cot = even4(halves(value), t_keep[s, 0])
        value_cot = even4(halves(key), t_keep[s, 1])
        mean = dot(beside(*halves(key_cot * key)), mean_weight) * (HEADS / D)
        return beside(scale[:, :D] * (key_cot - key * mean), scale[:, D:] * (value_cot - value * mean))

    early_route.start(0)

    def middle_back(index, _):
        @pl.when(index == 1)
        def _():
            mode_route.step(2)
            early_route.step(0)

        where = block(index)
        s = index // steps
        cot = norm_back(s, x_keep[where, :], r_keep[where, :])
        pieces = thirds(cot)
        high, low = pieces[:2]
        kept = h1_keep[where, :]
        kv_acc[...] += dot(kept, high, 0, 0)
        kv_acc[:D, :] += dot(kept[:, :D], low, 0, 0)
        out = d_keep[where, :]
        out = (
            out
            + even4(halves(out), nt_keep[s])
            + tall6(pieces, (w_kvt[:, : 2 * D], w_kvt[:, 2 * D :]))
        )
        outer, inner = feed_back(0, index, out)
        v_acc[s] += dot(lrows[index], beside(*outer[:2]))
        u_acc[s] += dot(lrows[index], beside(*inner[:2]))
        return 0

    lax.fori_loop(0, rows_all, middle_back, 0)
    mode_route.finish(3)
    put_mode.start()
    early_route.step(1)

    def lift_sum(value):
        value = fold(value)
        return above(
            value[0:1] + value[1:2] + value[2:3],
            value[3:4] + value[4:5] + value[5:6],
            value[6:7],
            jnp.zeros((5, value.shape[1]), F32),
        )

    inner_rows = [lift_sum(u_acc[s]) for s in range(count)]
    value_rows = [lift_sum(v_acc[s]) + exact(inner_rows[s], ffn_ref[0, 0], 1, 1) for s in range(count)]
    gains[0] = attend_back(0, [exact(lift_rows, value_rows[s], 0, 0) for s in range(count)])

    query_rows = jnp.zeros((8, D), F32)
    lift_part = jnp.zeros((8, D), F32)
    inner_grad = jnp.zeros((D, FF), F32)
    for s in range(count):
        query_rows += exact(value_rows[s], small_keep[0, s, 2], 1, 1)
        lift_part += value_rows[s] + exact(value_rows[s], n_keep[0, s], 1, 1)
        inner_grad += exact(mid_rows[s], inner_rows[s], 0, 0)
    for i in range(2):
        half = slice(i * D, (i + 1) * D)
        late[i * D : (i + 1) * D, :] = exact(kv_acc[:D, half] + kv_acc[D:, half], centre)
        late[(2 + i) * D : (3 + i) * D, :] = w2_acc[0, :D, half] + w2_acc[0, D:, half]
        late[(4 + i) * D : (5 + i) * D, :] = inner_grad[:, half]

    def bias(slot, width=D):
        return jnp.sum(b_acc[slot * 8 : slot * 8 + 8, :width], 0, keepdims=True)

    rows = [jnp.zeros((3, D), F32)]
    for layer in range(LAYERS):
        inner = bias(8 + 2 * layer, FF)
        rows += [gains[layer][0], gains[layer][1], inner[:, :D], inner[:, D:], bias(7 + 2 * layer)]
    short = [fold(bias(slot)) for slot in (6, 5, 4, 3, 2)]
    rows += [beside(short[0], short[1]), beside(short[2], short[3]), beside(short[4], jnp.zeros((1, FREQ), F32))]
    late[7 * D : 7 * D + 16, :] = above(*rows)
    lanes = lax.broadcasted_iota(jnp.int32, (1, D), 1)
    first = jnp.where(lax.rem(lanes, FREQ) == 0, bias(0), 0.0)
    second = jnp.where(lax.rem(lanes, FREQ) == 0, bias(1), 0.0)
    late[7 * D + 16 : 7 * D + 24, :] = above(first, second, jnp.zeros((6, D), F32))
    late[7 * D + 24 : 7 * D + 32, :] = query_rows
    late[7 * D + 32 : 7 * D + 40, :] = lift_part
    late[7 * D + 40 :, :] = jnp.zeros((D - 40, D), F32)
    late_route.start(0)

    def front_back(index, _):
        @pl.when(index == 1)
        def _():
            late_route.step(0)

        centred = dot(lifted[block(index), :], w0_kv[...])
        scale = head_scale(centred)
        cot = norm_back(index // steps, centred * scale, scale)
        vt_acc[...] += dot(lrows[index], beside(*halves(cot)))
        return 0

    lax.fori_loop(0, rows_all, front_back, 0)
    turned = lift_sum(vt_acc[...])
    tail_send[...] = above(turned[:4, :D], turned[:4, D:])
    swap = pltpu.make_async_remote_copy(
        src_ref=tail_send,
        dst_ref=tail_swap,
        send_sem=tail_sends.at[devices // 2 - 1],
        recv_sem=tail_recvs.at[devices // 2 - 1],
        device_id=device_of(x, 1 - core, z, y),
        device_id_type=MESH,
    )
    swap.start()
    late_route.step(1)
    swap.wait()
    tail_pair[...] = tail_send[...] + tail_swap[...]
    tail_land[place] = tail_pair[...]
    to_each(lambda r: tail_pair, tail_land, lambda r: r - 16 * core, mine, tail_sends, tail_recvs, devices // 2 - 1, True)
    early_route.step(2)
    early_route.finish(3)
    put_early.start()
    to_each(lambda r: tail_pair, tail_land, lambda r: r - 16 * core, mine, tail_sends, tail_recvs, devices // 2 - 1, False)
    late_route.step(2)
    late_route.finish(3)
    put_mode.wait()
    put_early.wait()
    summed = jnp.sum(tail_land[...], 0)
    zero = jnp.zeros((4, 2 * D), F32)
    turned = above(beside(summed[:4], summed[4:]), zero)
    joined = exact(lift_rows, turned, 0, 0)
    tail_out[:D, :] = exact(lift_rows, late_out[7 * D + 24 : 7 * D + 32, :], 0, 0)
    tail_out[D : 2 * D, :] = exact(joined[:, :D], centre)
    tail_out[2 * D : 3 * D, :] = exact(joined[:, D:], centre)
    tail_out[3 * D :, :] = late_out[7 * D + 32 : 7 * D + 40, :] + exact(turned, cent_keep[0], 1, 1)


def tables(points):
    order = np.arange(MODES)[:, None]
    angle = (order * np.arange(points)[None, :]) % points * (2.0 * math.pi / points)
    full = np.concatenate([np.cos(angle), np.sin(angle)], 0).astype(np.float32)
    kind = np.dtype(ml_dtypes.bfloat16)
    high = full.astype(kind)
    rest = full - high.astype(np.float32)
    middle = rest.astype(kind)
    low = (rest - middle.astype(np.float32)).astype(kind)
    zero = np.zeros((4 * MODES, points), kind)
    column = np.concatenate([high, middle, high, middle, high, low, zero], 0).T
    row = np.concatenate([high, middle], 0).reshape(4 * MODES, points // ROWS, ROWS).transpose(1, 0, 2)
    return np.ascontiguousarray(column), np.ascontiguousarray(row)


def summed_grads(samples_in, target, mask, attn_w, ffn_w, spec_w, turned_w, vectors):
    parts = samples_in.shape[0] // 2
    count, points = 2, samples_in.shape[2] * parts
    devices = FLAYERS * MODES
    total = count * points
    steps = points // ROWS
    column, row = tables(points)
    vmem = pl.BlockSpec(memory_space=pltpu.VMEM)
    anywhere = pl.BlockSpec(memory_space=pl.ANY)
    first = [
        ((parts, 8, samples_in.shape[2]), F32),
        ((parts, 8, samples_in.shape[2]), F32),
        ((NVEC_ROWS, D), F32),
        ((8 * D, D), F32),
        ((8 * D, D), F32),
        ((8 * D, D), F32),
        ((8 * D, D), F32),
        ((devices, 8, D), F32),
        ((devices, 8, D), F32),
        ((8, D), F32),
        ((8, D), F32),
        ((8, D), F32),
        ((devices // 2, 8, D), F32),
    ]
    numbers = (3 * devices, 3 * devices, parts - 1, parts - 1, devices - 1, devices - 1, devices // 2, devices // 2)
    scratch = [
        ((total, D), BF16),
        ((total // ROWS, 16, ROWS), BF16),
        ((6 * D, 2 * D), BF16),
        ((4 * D, 3 * D), BF16),
        ((6 * D, FF), BF16),
        ((2 * FF, 3 * D), BF16),
        ((count, D, FF), BF16),
        ((count, 8, D), F32),
        ((LAYERS, 2 * FF, 2 * D), BF16),
        ((LAYERS, 2 * FF, D), BF16),
        ((LAYERS, 6 * D, FF), BF16),
        ((total, 2 * D), F32),
        ((total, 2 * D), F32),
        ((LAYERS, total, FF), F32),
        ((LAYERS, total, 2 * FF), BF16),
        ((total, 2 * D), BF16),
        ((total, 2 * D), BF16),
        ((total, 3 * D), BF16),
        ((FLAYERS, points, 3 * D), BF16),
        ((points, 3 * D), BF16),
        ((count, 2 * D, 2 * D), F32),
        ((D, 2 * D), BF16),
        ((count, D, D), BF16),
        ((LAYERS, count, D, D), F32),
        ((LAYERS, count, 3, D, D), F32),
        ((count, 2 * D, 2 * D), BF16),
        ((LAYERS, D, 2 * D), F32),
        ((4 * MODES, 2 * D), F32),
        ((FLAYERS, 2 * count * MODES, D), F32),
        ((2 * D, D), BF16),
        ((3, 2 * D, 2 * D), F32),
        ((4 * D, 2 * D), F32),
        ((LAYERS, 2 * D, FF), F32),
        ((2 * D, FF), F32),
        ((2 * D, 2 * D), F32),
        ((count, 16, 2 * D), F32),
        ((count, 16, 2 * FF), F32),
        ((16, 4 * D), F32),
        ((96, FF), F32),
        ((total, D), F32),
        ((count, 2, 2 * D, 2 * D), BF16),
        ((count, 4 * D, 2 * D), BF16),
    ]
    shapes = [(8 * D, D), (8 * D, D), (devices * FREQ, D), (3 * D + 8, D)]
    return pl.pallas_call(
        step_kernel,
        out_shape=[jax.ShapeDtypeStruct(shape, F32) for shape in shapes],
        in_specs=[vmem] * 5 + [anywhere] + [vmem] * 2 + [anywhere] * 2,
        out_specs=[anywhere, vmem, anywhere, vmem],
        scratch_shapes=[
            pltpu.VMEM(spec_w.shape, F32),
            pltpu.VMEM(column.shape, BF16),
            pltpu.VMEM(row.shape, BF16),
            pltpu.VMEM(shapes[0], F32),
            pltpu.VMEM(shapes[2], F32),
            pltpu.SemaphoreType.DMA((5,)),
        ]
        + [pltpu.VMEM(*item) for item in first]
        + [pltpu.SemaphoreType.DMA((number,)) for number in numbers]
        + [pltpu.VMEM(*item) for item in scratch],
        compiler_params=pltpu.CompilerParams(
            vmem_limit_bytes=64 * 2**20 - 2**17, collective_id=0, has_side_effects=True
        ),
    )(
        samples_in,
        target,
        mask,
        attn_w,
        ffn_w,
        spec_w,
        turned_w,
        vectors,
        jnp.asarray(column),
        jnp.asarray(row),
    )


def update_kernel(
    early_any,
    late_any,
    modes_any,
    tail_any,
    vectors,
    vector_m,
    vector_v,
    attn_w,
    ffn_w,
    spec_w,
    turned_w,
    attn_m,
    ffn_m,
    spec_m,
    turned_m,
    attn_v,
    ffn_v,
    spec_v,
    turned_v,
    loss_out,
    count_out,
    weight_out,
    update_out,
    ratio_out,
    vector_m_out,
    vector_v_out,
    vector_w_out,
    vector_low_out,
    *rest,
):
    outs, scratch = rest[:16], rest[16:]
    ins = (attn_w, ffn_w, spec_w, turned_w, attn_m, ffn_m, spec_m, turned_m, attn_v, ffn_v, spec_v, turned_v)
    held, fresh = scratch[:12], scratch[12:28]
    flat, in_sems, out_sems, early, late, modes, tail, grad_sems = scratch[28:]

    blocks = [(2, 0), (2, 1), (1, 1), (1, 0), (0, 1), (0, 0), (3, None)]

    def view(ref, part):
        return ref if part is None else ref.at[part]

    def load(slot, kind):
        array, part = blocks[slot]
        number = kind * 4 + array
        return pltpu.make_async_copy(
            view(ins[number], part), view(held[number], part), in_sems.at[slot * 3 + kind]
        )

    def store(slot, kind):
        array, part = blocks[slot]
        number = kind * 4 + array
        return pltpu.make_async_copy(
            view(fresh[number], part), view(outs[number], part), out_sems.at[slot * 4 + kind]
        )

    grads = [
        pltpu.make_async_copy(source, target, grad_sems.at[i])
        for i, (source, target) in enumerate(
            ((late_any, late), (tail_any, tail), (modes_any, modes), (early_any, early))
        )
    ]
    for copy in grads[:3]:
        copy.start()
    for kind in range(3):
        load(0, kind).start()
    grads[3].start()
    for slot in range(1, len(blocks)):
        for kind in range(3):
            load(slot, kind).start()
    grads[0].wait()
    grads[1].wait()
    misc = late[7 * D + 16 : 7 * D + 24, :]
    loss_out[0] = jnp.sum(misc[0:1])
    valid = jnp.sum(misc[1:2], keepdims=True)
    count_out[0] = jnp.sum(misc[1:2])
    scale = 1.0 / valid

    def moved(weight, grad, first, second):
        first_new = BETA_ONE * first + (1.0 - BETA_ONE) * grad
        second_new = BETA_TWO * second + (1.0 - BETA_TWO) * grad * grad
        update = (
            first_new
            / (1.0 - BETA_ONE**STEP)
            / (jnp.sqrt(second_new / (1.0 - BETA_TWO**STEP)) + ADAM_EPS)
            + DECAY * weight
        )
        return first_new, second_new, update

    def note(slot, weight_sum, update_sum):
        weight_norm, update_norm = jnp.sqrt(weight_sum), jnp.sqrt(update_sum)
        ratio = weight_norm / (update_norm + ADAM_EPS)
        weight_out[slot] = weight_norm[0, 0]
        update_out[slot] = update_norm[0, 0]
        ratio_out[slot] = ratio[0, 0]
        return RATE * ratio

    def total(sums):
        return sum(jnp.sum(value, keepdims=True) for value in sums.values())

    for i in range(NVEC_ROWS):
        start = i * D
        size = min(D, flat.shape[0] - start)
        row = tail[3 * D + i : 3 * D + i + 1, :] if i < 3 else late[7 * D + i : 7 * D + i + 1, :]
        flat[start : start + size] = (row * scale)[:, :size].reshape(size)
    weight = vectors[...]
    first_new, second_new, update = moved(weight, flat[...], vector_m[...], vector_v[...])
    vector_m_out[...] = first_new
    vector_v_out[...] = second_new
    rate = note(
        7,
        jnp.sum(weight * weight).reshape(1, 1),
        jnp.sum(update * update).reshape(1, 1),
    )
    flat[...] = jnp.broadcast_to(rate, (1, D)).reshape(D)[0] * update
    weight = weight - flat[...]
    vector_w_out[...] = weight
    vector_low_out[...] = weight.astype(BF16)

    def grad_blocks(array, part):
        if array == 0:
            if part:
                places = [(early, 5 * D + FREQ), (late, 0), (late, D), (early, 6 * D + FREQ)]
            else:
                places = [(tail, 0), (tail, D), (tail, 2 * D), (late, 6 * D)]
            return [
                (ref, start, D, 0, (slice(None), slice(j * D, (j + 1) * D)))
                for j, (ref, start) in enumerate(places)
            ]
        if array == 1:
            ref, starts = (early, (0, 1, 2, 3)) if part else (late, (4, 5, 2, 3))
            return [
                (ref, starts[j] * D, D, 0, (j // 2, slice(None), slice(j % 2 * D, j % 2 * D + D)))
                for j in range(4)
            ]
        if array == 3:
            return [
                (early, 4 * D, FREQ, 0, (slice(None), slice(0, D))),
                (early, 4 * D + FREQ, FREQ, 0, (slice(None), slice(D, 2 * D))),
                (early, 5 * D, FREQ, 0, (slice(None), slice(2 * D, 2 * D + FREQ))),
            ]
        return [
            (modes, (part * MODES + k) * FREQ, FREQ, j * FREQ, (k, j))
            for k in range(MODES)
            for j in range(2)
        ]

    grads[2].wait()
    grads[3].wait()
    for slot, (array, part) in enumerate(blocks):
        for kind in range(3):
            load(slot, kind).wait()
        weight_ref, first_ref, second_ref = [view(held[kind * 4 + array], part) for kind in range(3)]
        first_out, second_out, weight_new, low_out = [view(fresh[kind * 4 + array], part) for kind in range(4)]
        pieces = grad_blocks(array, part)
        weight_sums, update_sums = {}, {}
        for ref, start, rows, lane, where in pieces:
            weight = weight_ref[where]
            width = weight.shape[1]
            grad = ref[start : start + rows, lane : lane + width] * scale
            first_new, second_new, update = moved(weight, grad, first_ref[where], second_ref[where])
            first_out[where] = first_new
            second_out[where] = second_new
            weight_new[where] = update
            weight_sums[width] = weight_sums.get(width, 0.0) + column_sum(weight * weight)
            update_sums[width] = update_sums.get(width, 0.0) + column_sum(update * update)
        store(slot, 0).start()
        store(slot, 1).start()
        place = (0 + part if array == 0 else 2 + part if array == 1 else 4 + part) if part is not None else 6
        rate = note(place, total(weight_sums), total(update_sums))
        for ref, start, rows, lane, where in pieces:
            weight = weight_ref[where] - rate * weight_new[where]
            weight_new[where] = weight
            low_out[where] = weight.astype(BF16)
        store(slot, 2).start()
        store(slot, 3).start()
    for slot in range(len(blocks)):
        for kind in range(4):
            store(slot, kind).wait()


def fast_body(samples_in, target, mask, attn_w, ffn_w, spec_w, dense_w, vectors, *moments):
    flat_spec = spec_w.reshape(FLAYERS, MODES * 2 * FREQ, FREQ)
    grads = summed_grads(samples_in, target, mask, attn_w, ffn_w, flat_spec, dense_w.T, vectors)
    sets = [
        (attn_w, ffn_w, spec_w, dense_w.T),
        (moments[0], moments[1], moments[2], moments[3].T),
        (moments[5], moments[6], moments[7], moments[8].T),
    ]
    vmem = pl.BlockSpec(memory_space=pltpu.VMEM)
    smem = pl.BlockSpec(memory_space=pltpu.SMEM)
    anywhere = pl.BlockSpec(memory_space=pl.ANY)
    shapes = [item.shape for item in sets[0]]
    kinds = (F32, F32, F32, BF16)
    scalar = [jax.ShapeDtypeStruct((1,), F32)] * 2 + [jax.ShapeDtypeStruct((8,), F32)] * 3
    line = [jax.ShapeDtypeStruct(vectors.shape, kind) for kind in kinds]
    arrays = [jax.ShapeDtypeStruct(shape, kind) for kind in kinds for shape in shapes]
    out = pl.pallas_call(
        update_kernel,
        out_shape=scalar + line + arrays,
        in_specs=[anywhere] * 4 + [vmem] * 3 + [anywhere] * 12,
        out_specs=[smem] * 5 + [vmem] * 4 + [anywhere] * 16,
        scratch_shapes=[pltpu.VMEM(shape, F32) for _ in range(3) for shape in shapes]
        + [pltpu.VMEM(shape, kind) for kind in kinds for shape in shapes]
        + [pltpu.VMEM(vectors.shape, F32), pltpu.SemaphoreType.DMA((21,)), pltpu.SemaphoreType.DMA((28,))]
        + [pltpu.VMEM(grad.shape, F32) for grad in grads]
        + [pltpu.SemaphoreType.DMA((4,))],
        compiler_params=pltpu.CompilerParams(vmem_limit_bytes=60 * 2**20),
    )(*grads, vectors, moments[4], moments[9], *sets[0], *sets[1], *sets[2])
    loss_sum, valid_count, weight_norms, update_norms, ratios = out[:5]
    line, arrays = out[5:9], out[9:]
    results = [loss_sum.reshape(()), valid_count.reshape(())]
    for array in range(4):
        for kind in range(4):
            item = arrays[kind * 4 + array]
            results.append(item.T if array == 3 else item)
    return tuple(results + list(line) + [weight_norms, update_norms, ratios])


def choose_body(*arrays):
    samples_in = arrays[0]
    dp, parts = lax.axis_size("dp"), lax.axis_size("pts")
    fits = dp * parts == FLAYERS * MODES and dp == 4 and samples_in.shape[0] == 2 * parts
    return (fast_body if fits and samples_in.shape[2] * parts % WIDE == 0 else body)(*arrays)


def solution(mesh):
    placed = (
        P("dp", None, "pts"),
        P("dp", "pts"),
        P("dp", "pts"),
        P(),
        P(),
        P(),
        P(),
        P(),
        P(),
        P(),
        P(),
        P(),
        P(),
        P(),
        P(),
        P(),
        P(),
        P(),
    )
    return jax.shard_map(
        choose_body,
        mesh=mesh,
        in_specs=placed,
        out_specs=(
            P(),
            P(),
            P(),
            P(),
            P(),
            P(),
            P(),
            P(),
            P(),
            P(),
            P(),
            P(),
            P(),
            P(),
            P(),
            P(),
            P(),
            P(),
            P(),
            P(),
            P(),
            P(),
            P(),
            P(),
            P(),
        ),
        check_vma=False,
    )
```

profile of v0, /device:TPU:0, one launch (start us, length us, event | category | flops | bytes accessed | tf_op | source)
XLA Modules:
  0.0 123.2 jit_solution(13219779188052286883)
XLA Ops:
  0.7 110.0 %shard_map.387 = (f32[1024,128]{1,0:T(8,128)}, f32[1024,128]{1,0:T(8,128)}, f32[2048,128]{1,0:T(8,128)}, f32[392,128]{1,0:T(8,128)}) custom-call(f32[16,2,256]{2,1,0:T(2,128)} %samples_ref.1, f32[16,256]{1,0:T(8,128)} %target_ref.1, s32[16,256]{1,0:T(8,128)} %mask_ref.1, f32[2,128,512]{2,1,0:T(8,128)} %attn_w.1, f32[2,2,128,256]{3,2,1,0:T(8,128)} %ffn_w.1, ...), custom_call_target="tpu_custom_call" | custom-call | tf_op jit(solution)/shard_map/pallas_call | solution.py:1413
  110.7 12.3 %shard_map.388 = (f32[1]{0:T(128)}, f32[1]{0:T(128)}, f32[8]{0:T(128)}, f32[8]{0:T(128)}, f32[8]{0:T(128)}, /*index=5*/f32[1984]{0:T(1024)}, f32[1984]{0:T(1024)...) custom-call(f32[1024,128]{1,0:T(8,128)} %get-tuple-element.54.early_, ...), custom_call_target="tpu_custom_call" | custom-call | tf_op jit(solution)/shard_map/pallas_call | solution.py:1642
where the time goes:
time: 123 us
  Pallas kernels  122 us (99%)
    pallas_call x1, Pallas kernels, summed_grads(): pl.pallas_call(step_kernel, out_shape=[jax.ShapeDtypeStruct(shape, F32) f...  110 us
    pallas_call x1, Pallas kernels, fast_body(): pl.pallas_call(update_kernel, out_shape=scalar + line + arrays, in_specs=...  12.3 us

commit v1 on v0

--- a/solution.py
+++ b/solution.py
@@ -1444,10 +1444,10 @@
 
 
 def update_kernel(
-    early_any,
-    late_any,
-    modes_any,
-    tail_any,
+    early,
+    late,
+    modes,
+    tail,
     vectors,
     vector_m,
     vector_v,
@@ -1477,9 +1477,9 @@
     outs, scratch = rest[:16], rest[16:]
     ins = (attn_w, ffn_w, spec_w, turned_w, attn_m, ffn_m, spec_m, turned_m, attn_v, ffn_v, spec_v, turned_v)
     held, fresh = scratch[:12], scratch[12:28]
-    flat, in_sems, out_sems, early, late, modes, tail, grad_sems = scratch[28:]
-
-    blocks = [(2, 0), (2, 1), (1, 1), (1, 0), (0, 1), (0, 0), (3, None)]
+    flat, in_sems, out_sems = scratch[28:]
+
+    blocks = [(2, 0), (2, 1), (1, 1), (0, 1), (0, 0), (1, 0), (3, None)]
 
     def view(ref, part):
         return ref if part is None else ref.at[part]
@@ -1498,22 +1498,9 @@
             view(fresh[number], part), view(outs[number], part), out_sems.at[slot * 4 + kind]
         )
 
-    grads = [
-        pltpu.make_async_copy(source, target, grad_sems.at[i])
-        for i, (source, target) in enumerate(
-            ((late_any, late), (tail_any, tail), (modes_any, modes), (early_any, early))
-        )
-    ]
-    for copy in grads[:3]:
-        copy.start()
-    for kind in range(3):
-        load(0, kind).start()
-    grads[3].start()
-    for slot in range(1, len(blocks)):
+    for slot in range(len(blocks)):
         for kind in range(3):
             load(slot, kind).start()
-    grads[0].wait()
-    grads[1].wait()
     misc = late[7 * D + 16 : 7 * D + 24, :]
     loss_out[0] = jnp.sum(misc[0:1])
     valid = jnp.sum(misc[1:2], keepdims=True)
@@ -1589,8 +1576,6 @@
             for j in range(2)
         ]
 
-    grads[2].wait()
-    grads[3].wait()
     for slot, (array, part) in enumerate(blocks):
         for kind in range(3):
             load(slot, kind).wait()
@@ -1642,13 +1627,11 @@
     out = pl.pallas_call(
         update_kernel,
         out_shape=scalar + line + arrays,
-        in_specs=[anywhere] * 4 + [vmem] * 3 + [anywhere] * 12,
+        in_specs=[vmem] * 7 + [anywhere] * 12,
         out_specs=[smem] * 5 + [vmem] * 4 + [anywhere] * 16,
         scratch_shapes=[pltpu.VMEM(shape, F32) for _ in range(3) for shape in shapes]
         + [pltpu.VMEM(shape, kind) for kind in kinds for shape in shapes]
-        + [pltpu.VMEM(vectors.shape, F32), pltpu.SemaphoreType.DMA((21,)), pltpu.SemaphoreType.DMA((28,))]
-        + [pltpu.VMEM(grad.shape, F32) for grad in grads]
-        + [pltpu.SemaphoreType.DMA((4,))],
+        + [pltpu.VMEM(vectors.shape, F32), pltpu.SemaphoreType.DMA((21,)), pltpu.SemaphoreType.DMA((28,))],
         compiler_params=pltpu.CompilerParams(vmem_limit_bytes=60 * 2**20),
     )(*grads, vectors, moments[4], moments[9], *sets[0], *sets[1], *sets[2])
     loss_sum, valid_count, weight_norms, update_norms, ratios = out[:5]

time: 123 us -> 122 us (level)
    pallas_call x1, Pallas kernels: 12.3 us -> 10.6 us  [fast_body(): pl.pallas_call(update_kernel, out_shape=scalar + line + arrays, in_specs=...]
where the time goes in v1:
time: 122 us
  Pallas kernels  121 us (99%)
    pallas_call x1, Pallas kernels, summed_grads(): pl.pallas_call(step_kernel, out_shape=[jax.ShapeDtypeStruct(shape, F32) f...  110 us
    pallas_call x1, Pallas kernels, fast_body(): pl.pallas_call(update_kernel, out_shape=scalar + line + arrays, in_specs=...  10.6 us

profile of v1, /device:TPU:0, one launch (start us, length us, event | category | flops | bytes accessed | tf_op | source)
XLA Modules:
  0.0 121.5 jit_solution(15469344402511550018)
XLA Ops:
  0.7 110.0 %shard_map.387 = (f32[1024,128]{1,0:T(8,128)}, f32[1024,128]{1,0:T(8,128)}, f32[2048,128]{1,0:T(8,128)}, f32[392,128]{1,0:T(8,128)}) custom-call(f32[16,2,256]{2,1,0:T(2,128)} %samples_ref.1, f32[16,256]{1,0:T(8,128)} %target_ref.1, s32[16,256]{1,0:T(8,128)} %mask_ref.1, f32[2,128,512]{2,1,0:T(8,128)} %attn_w.1, f32[2,2,128,256]{3,2,1,0:T(8,128)} %ffn_w.1, ...), custom_call_target="tpu_custom_call" | custom-call | tf_op jit(solution)/shard_map/pallas_call | solution.py:1413
  110.7 10.6 %shard_map.388 = (f32[1]{0:T(128)}, f32[1]{0:T(128)}, f32[8]{0:T(128)}, f32[8]{0:T(128)}, f32[8]{0:T(128)}, /*index=5*/f32[1984]{0:T(1024)}, f32[1984]{0:T(1024)...) custom-call(f32[1024,128]{1,0:T(8,128)} %get-tuple-element.54.early,, ...), custom_call_target="tpu_custom_call" | custom-call | tf_op jit(solution)/shard_map/pallas_call | solution.py:1627
